TPU v7x, 32 devices: a whole 2x2x4 slice. The times are simulated.
32 devices in a mesh: band: 4 (over y, x), pix: 8 (over z, core).
Axes of the slice: x: 2, y: 2, z: 4, core: 2. Of those that a mesh axis runs over, the one named last changes fastest.
Arguments:
- radiance: float32 [256, 1920], P('pix', 'band'), may hold values from -6 to 6
- stem_weight: float32 [32, 1024], replicated, may hold values from -1 to 1
- band_embed: float32 [120, 1024], replicated, may hold values from -4 to 4
- norm_spectral: float32 [1024], replicated, may hold values from 0.1 to 1.9
- spec_qkv: bfloat16 [1024, 3072], replicated, as said below
- spec_out: bfloat16 [1024, 1024], replicated, may hold values from -0.1875 to 0.1875
- norm_spatial: float32 [1024], replicated, may hold values from 0.1 to 1.9
- spat_qkv: bfloat16 [1024, 3072], replicated, as said below
- spat_out: bfloat16 [1024, 1024], replicated, may hold values from -0.1875 to 0.1875
- norm_mlp: float32 [1024], replicated, may hold values from 0.1 to 1.9
- up_weight: bfloat16 [4096, 1024], P('pix'), may hold values from -0.1875 to 0.1875
- up_bias: bfloat16 [4096], P('pix'), may hold values from -3 to 3
- down_weight: bfloat16 [4096, 1024], P('pix'), may hold values from -0.09375 to 0.09375
Outputs:
- encoded: bfloat16 [256, 120, 1024], P(('pix', 'band'))
Inputs may be any that keep to these rules, and one draw needn't show every extreme that they name: `spec_qkv`: columns ordered by head, then query, key, value, then head entries. `spat_qkv`: columns ordered by head, then query, key, value, then head entries.
All inputs are finite; a program needn't handle non-finite values.
Results may differ from a plain program's by a relative error of at most 0.009.
Values may be sent and summed in bfloat16 or wider, within the bound.
No kernel may reach another device: no remote copies, remote signals or barrier semaphores. Data moves between devices by JAX's collectives and lax.ppermute only.
A program may use at most 128 MiB of HBM per device.

v0:
```python
import jax
import jax.numpy as jnp
from jax import lax
from jax.sharding import PartitionSpec as P

HEADS = 16
CH_TOK = 16


def padded_2(cells, sides, width):
    for axis, dim in sides:
        count = lax.axis_size(axis)
        ends = count - 1
        head = lax.slice_in_dim(cells, 0, width, axis=dim)
        tail = lax.slice_in_dim(cells, cells.shape[dim] - width, cells.shape[dim], axis=dim)
        cells = jnp.concatenate(
            [
                lax.ppermute(tail, axis, [(i, (i + 1) % count) for i in range(ends)]),
                cells,
                lax.ppermute(head, axis, [((i + 1) % count, i) for i in range(ends)]),
            ],
            axis=dim,
        )
    return cells


def layer_norm(values, scaling):
    values = values.astype(jnp.float32)
    average = jnp.mean(values, axis=-1, keepdims=True)
    centred = values - average
    variance = jnp.mean(centred * centred, axis=-1, keepdims=True)
    return centred * lax.rsqrt(variance + 1e-05) * scaling


def attend(queries, key_rows, value_rows, form_scores, form_mix):
    scale = queries.shape[-1] ** (-0.5)
    scores = jnp.einsum(form_scores, queries, key_rows, preferred_element_type=jnp.float32) * scale
    scores = scores - jnp.max(scores, axis=-1, keepdims=True)
    weights = jnp.exp(scores)
    weights = weights / jnp.sum(weights, axis=-1, keepdims=True)
    probabilities = weights.astype(jnp.bfloat16)
    mixed = jnp.einsum(form_mix, probabilities, value_rows, preferred_element_type=jnp.float32)
    return mixed.astype(jnp.bfloat16)


def embed_windows(padded, stem_weight, embedding):
    row_count, width = padded.shape
    band_count = width // CH_TOK - 1
    blocks = padded.reshape(row_count, band_count + 1, CH_TOK)
    windows = jnp.concatenate([blocks[:, :-1], blocks[:, 1:]], axis=2).reshape(
        row_count * band_count, 2 * CH_TOK
    )
    result = jnp.dot(
        windows, stem_weight, precision=lax.Precision.HIGHEST, preferred_element_type=jnp.float32
    )
    result = result.reshape(row_count, band_count, -1) + embedding[None]
    return result.astype(jnp.bfloat16)


def local(
    radiance,
    stem_weight,
    band_embed,
    norm_spectral,
    spec_qkv,
    spec_out,
    norm_spatial,
    spat_qkv,
    spat_out,
    norm_mlp,
    up_weight,
    up_bias,
    down_weight,
):
    half_reach = CH_TOK // 2
    padded = padded_2(radiance, (("band", 1),), half_reach)
    bands_here = radiance.shape[1] // CH_TOK
    offset = lax.axis_index("band") * bands_here
    embedding = lax.dynamic_slice_in_dim(band_embed, offset, bands_here, 0)
    local_tokens = embed_windows(padded, stem_weight, embedding)
    tokens = lax.all_to_all(local_tokens, "band", split_axis=0, concat_axis=1, tiled=True)
    pixel_count, band_count, width = tokens.shape
    head_dim = width // HEADS
    normed = layer_norm(tokens, norm_spectral).astype(jnp.bfloat16).reshape(-1, width)
    projected = jnp.dot(normed, spec_qkv, preferred_element_type=jnp.float32).astype(jnp.bfloat16)
    projected = projected.reshape(pixel_count, band_count, HEADS, 3, head_dim)
    spectral_mix = attend(
        projected[:, :, :, 0],
        projected[:, :, :, 1],
        projected[:, :, :, 2],
        "pqhd,pkhd->phqk",
        "phqk,pkhd->pqhd",
    )
    after_spectral = tokens.reshape(-1, width).astype(jnp.float32) + jnp.dot(
        spectral_mix.reshape(-1, width), spec_out, preferred_element_type=jnp.float32
    )
    spatial_in = layer_norm(after_spectral, norm_spatial).astype(jnp.bfloat16)
    spatial_proj = jnp.dot(spatial_in, spat_qkv, preferred_element_type=jnp.float32).astype(
        jnp.bfloat16
    )
    group_count = lax.axis_size(("band", "pix"))
    items_each = band_count * HEADS // group_count
    spatial_proj = spatial_proj.reshape(pixel_count, group_count, items_each, 3 * head_dim)
    per_item = jnp.moveaxis(
        lax.all_to_all(spatial_proj, ("band", "pix"), split_axis=1, concat_axis=0, tiled=True)[
            :, 0
        ],
        1,
        0,
    )

    def one_item(rows):
        return attend(
            rows[:, :head_dim],
            rows[:, head_dim : 2 * head_dim],
            rows[:, 2 * head_dim :],
            "qd,kd->qk",
            "qk,kd->qd",
        )

    attended = jnp.moveaxis(lax.map(one_item, per_item), 0, 1)[:, None]
    returned = lax.all_to_all(attended, ("band", "pix"), split_axis=0, concat_axis=1, tiled=True)
    after_spatial = after_spectral + jnp.dot(
        returned.reshape(-1, width), spat_out, preferred_element_type=jnp.float32
    )
    mlp_in = layer_norm(after_spatial, norm_mlp).astype(jnp.bfloat16)
    up_piece = lax.all_gather(up_weight, "pix", axis=0, tiled=True)
    bias_piece = lax.all_gather(up_bias, "pix", axis=0, tiled=True)
    down_piece = lax.all_gather(down_weight, "pix", axis=0, tiled=True)
    pre_act = lax.dot_general(
        mlp_in, up_piece, (((1,), (1,)), ((), ())), preferred_element_type=jnp.float32
    )
    pre_act = pre_act + bias_piece.astype(jnp.float32)
    hidden = jax.nn.gelu(pre_act, approximate=True).astype(jnp.bfloat16)
    feed_forward = jnp.dot(hidden, down_piece, preferred_element_type=jnp.float32)
    encoded = (after_spatial + feed_forward).astype(jnp.bfloat16)
    return encoded.reshape(pixel_count, band_count, width)


def solution(mesh):
    placed = (
        P("pix", "band"),
        P(),
        P(),
        P(),
        P(),
        P(),
        P(),
        P(),
        P(),
        P(),
        P("pix", None),
        P("pix"),
        P("pix", None),
    )
    return jax.shard_map(
        local, mesh=mesh, in_specs=placed, out_specs=P(("pix", "band"), None, None), check_vma=False
    )
```

profile of v0, /device:TPU:0, one launch (start us, length us, event | category | flops | bytes accessed | tf_op | source)
XLA Modules:
  0.0 675.4 jit_solution(15414650013233634329)
XLA Ops:
  7.5 4.8 collective-permute-start
  14.6 3.4 collective-permute-done.1
  19.5 4.2 add_convert_fusion.1
  26.2 4.5 all-to-all-start
  31.4 23.7 %all-to-all-done = bf16[32,30,1024]{2,1,0:T(8,128)(2,1)} async-done(((bf16[32,30,1024]{2,1,0:T(8,128)(2,1)}), bf16[32,30,1024]{2,1,0:T(8,128)(2,1)}, u32[]{:S(2)}, u32[]{:S(2)}) %all-to-all-start) | async-done | bytes 1966112 | tf_op jit(solution)/shard_map/all_to_all | solution.py:81
  58.4 4.1 copy_bitcast_fusion.1
  62.4 4.8 reshape.106
  67.2 11.4 %convolution_convert_fusion.2 = bf16[960,3072]{1,0:T(8,128)(2,1)} fusion(bf16[1024,3072]{1,0:T(8,128)(2,1)} %param.19, f32[960,1024]{1,0:T(8,128)} %reshape.106, f32[1024]{0:T(1024)S(1)} %copy-done.5, f32[960]{0:T(1024)S(1)} %rsqrt.28, f32[960]{0:T(1024)S(1)} %div.37), kind=kOutput, calls=%fused_computation.31 | convolution fusion | flops 6046679040 | bytes 16133632 | tf_op jit(solution)/shard_map/dot_general | solution.py:85
  78.6 8.5 %copy.54 = bf16[960,3072]{0,1:T(8,128)(2,1)} copy(bf16[960,3072]{1,0:T(8,128)(2,1)} %convolution_convert_fusion.2) | data formatting | bytes 11796480 | tf_op jit(solution)/shard_map/convert_element_type | solution.py:85
  87.1 12.7 %reshape.101 = bf16[8,120,16,3,64]{1,0,4,3,2:T(8,128)(2,1)} reshape(bf16[960,3072]{0,1:T(8,128)(2,1)} %copy.54) | data formatting | bytes 11796480 | tf_op jit(solution)/shard_map/reshape | solution.py:86
  99.8 3.6 fusion.53
  105.7 7.8 %fusion.56 = (f32[8,16,120]{2,1,0:T(8,128)S(1)}, f32[8,16,120,120]{2,3,1,0:T(8,128)S(1)}) fusion(f32[8,16,120,120]{2,3,1,0:T(8,128)S(1)} %fusion.28), kind=kOutput, calls=%fused_computation.83 | output fusion | flops 7372919 | bytes 14807040 | tf_op jit(solution)/shard_map/sub | solution.py:38
  115.0 3.1 copy.59
  118.1 5.1 reshape.102
  123.2 5.3 fusion.57
  130.4 11.2 %convolution_convert_fusion.1 = bf16[960,3072]{1,0:T(8,128)(2,1)} fusion(bf16[1024,3072]{1,0:T(8,128)(2,1)} %param.22, f32[960,1024]{1,0:T(8,128)S(1)} %get-tuple-element.41, f32[1024]{0:T(1024)S(1)} %copy-done.6, f32[960]{0:T(1024)S(1)} %add_rsqrt_fusion.2, f32[960]{0:T(1024)S(1)} %broadcast_multiply_fusion.2), kind=kOutput, calls=%fused_computation.30 | convolution fusion | flops 6046679040 | bytes 16133632 | tf_op jit(solution)/shard_map/dot_general | solution.py:98
  141.6 12.5 %reshape.103 = bf16[8,32,60,192]{3,2,1,0:T(8,128)(2,1)} reshape(bf16[960,3072]{1,0:T(8,128)(2,1)} %convolution_convert_fusion.1) | data formatting | bytes 11796480 | tf_op jit(solution)/shard_map/reshape | solution.py:103
  154.1 14.5 %copy.60 = bf16[8,32,60,192]{3,0,2,1:T(8,128)(2,1)} copy(bf16[8,32,60,192]{3,2,1,0:T(8,128)(2,1)} %reshape.103) | data formatting | bytes 11796480 | tf_op jit(solution)/shard_map/reshape | solution.py:103
  168.6 5.1 all-to-all-start.1
  174.5 240.3 %all-to-all-done.1 = bf16[8,32,60,192]{3,0,2,1:T(8,128)(2,1)} async-done(((bf16[8,32,60,192]{3,0,2,1:T(8,128)(2,1)}), bf16[8,32,60,192]{3,0,2,1:T(8,128)(2,1)}, u32[]{:S(2)}, u32[]{:S(2)}) %all-to-all-start.1) | async-done | bytes 5898272 | tf_op jit(solution)/shard_map/all_to_all | solution.py:105
  414.7 7.3 %copy_bitcast_fusion = bf16[60,256,192]{2,1,0:T(8,128)(2,1)} fusion(bf16[8,32,60,192]{3,0,2,1:T(8,128)(2,1)} %all-to-all-done.1), kind=kLoop, calls=%fused_computation.23 | loop fusion | bytes 11796480 | tf_op jit(solution)/shard_map/transpose | solution.py:104
  422.1 124.3 %while.10 = (s32[]{:T(128)}, bf16[60,256,64]{1,2,0:T(8,128)(2,1)}, bf16[60,256,192]{2,1,0:T(8,128)(2,1)}, s32[]{:T(128)}) while((s32[]{:T(128)}, bf16[60,256,64]{1,2,0:T(8,128)(2,1)}, bf16[60,256,192]{2,1,0:T(8,128)(2,1)}, s32[]{:T(128)}) %tuple.28), condition=%wide.region_9.10_spmd, body=%wide.region_6.9_spmd.sunk | while | flops 17251840 | bytes 1185337 | solution.py:121
  546.4 7.4 %copy.62 = bf16[60,256,64]{2,0,1:T(8,128)(2,1)} copy(bf16[60,256,64]{1,2,0:T(8,128)(2,1)} %get-tuple-element.22) | data formatting | bytes 3932160 | tf_op jit(solution)/shard_map/while | solution.py:121
  553.8 7.8 %reshape.113 = bf16[32,2,15360]{2,1,0:T(2,128)(2,1)} reshape(bf16[256,1,60,64]{3,2,1,0:T(8,128)(2,1)} %bitcast.72) | data formatting | bytes 3932160
  561.6 2.9 all-to-all-start.2
  564.5 51.8 %all-gather = bf16[8,1,512]{2,1,0:T(2,128)(2,1)S(1)} all-gather(bf16[1,1,512]{2,1,0:T(2,128)(2,1)S(1)} %reshape.109), channel_id=1, replica_groups=mesh['band'=4,'pix'=8] {'pix'}, dimensions={0}, use_global_device_ids=true | all-gather | bytes 9216 | tf_op jit(solution)/shard_map/all_gather | solution.py:128
  616.3 4.0 reshape.114
  620.3 4.7 copy.86
  625.0 4.5 copy.64
  629.5 4.7 reshape.104
  634.2 5.0 fusion.58
  641.8 26.6 %add_convert_fusion = bf16[960,1024]{1,0:T(8,128)(2,1)} fusion(f32[960,1024]{1,0:T(8,128)} %copy-done.3, bf16[4096,1024]{1,0:T(8,128)(2,1)} %all-gather.6.cloned.1.call-done, f32[4096]{0:T(1024)S(1)} %bitcast.75, bf16[4096,1024]{1,0:T(8,128)(2,1)} %all-gather.4.cloned.1.call-done, f32[1024]{0:T(1024)S(1)} %copy-done.7, f32[960]{0:T(1024)S(1)} %add_rsqrt_fusion.1, ...), kind=kOutput, calls=%fused_computation.35 | convolution fusion | flops 16151347200 | bytes 22703616 | tf_op jit(solution)/shard_map/dot_general | solution.py:135
  (291 shorter events, 143.7 us)
Async XLA Ops:
  6.5 116.6 %copy-start = (bf16[1024,1024]{1,0:T(8,128)(2,1)S(1)}, bf16[1024,1024]{1,0:T(8,128)(2,1)}, u32[]{:S(2)}) copy-start(bf16[1024,1024]{1,0:T(8,128)(2,1)} %param.20) | copy-start | bytes 6291460
  7.5 7.1 %collective-permute-start = (f32[32,8]{1,0:T(8,128)S(1)}, f32[32,8]{1,0:T(8,128)S(1)}, u32[]{:S(2)}, u32[]{:S(2)}) collective-permute-start(f32[32,8]{1,0:T(8,128)S(1)} %get-tuple-element.36), channel_id=1, source_target_pairs={{0,8},{8,16},{16,24},{1,9},{9,17},{17,25},{2,10},{10,18},{18,26},{... | collective-permute-start | bytes 3080 | tf_op jit(solution)/shard_map/ppermute | solution.py:18
  12.3 5.6 collective-permute-start.1
  26.2 28.9 %all-to-all-start = ((bf16[32,30,1024]{2,1,0:T(8,128)(2,1)}), bf16[32,30,1024]{2,1,0:T(8,128)(2,1)}, u32[]{:S(2)}, u32[]{:S(2)}) async-start(bf16[32,30,1024]{2,1,0:T(8,128)(2,1)} %copy.52), calls=%async_computation | async-start | bytes 4194304 | tf_op jit(solution)/shard_map/all_to_all | solution.py:81
  30.7 611.0 %all-gather.4.cloned.1.call-start = ((), (), s32[]{:S(2)}) async-start(), calls=%async_computation.3 | async-start | bytes 9437184 | tf_op jit(solution)/shard_map/all_gather | solution.py:127
  62.4 4.8 copy-start.5
  128.5 1.9 copy-start.2
  128.5 1.9 copy-start.6
  168.6 246.1 %all-to-all-start.1 = ((bf16[8,32,60,192]{3,0,2,1:T(8,128)(2,1)}), bf16[8,32,60,192]{3,0,2,1:T(8,128)(2,1)}, u32[]{:S(2)}, u32[]{:S(2)}) async-start(bf16[8,32,60,192]{3,0,2,1:T(8,128)(2,1)} %copy.60), calls=%async_computation.1 | async-start | bytes 15728640 | tf_op jit(solution)/shard_map/all_to_all | solution.py:105
  173.7 468.1 %all-gather.6.cloned.1.call-start = ((), (), s32[]{:S(2)}) async-start(), calls=%async_computation.4 | async-start | bytes 9437184 | tf_op jit(solution)/shard_map/all_gather | solution.py:129
  553.8 10.7 %copy-start.4 = (bf16[512]{0:T(512)(128)(2,1)S(1)}, bf16[512]{0:T(512)(128)(2,1)}, u32[]{:S(2)}) copy-start(bf16[512]{0:T(512)(128)(2,1)} %param.26) | copy-start | bytes 3076
  561.6 54.7 %all-to-all-start.2 = ((bf16[32,2,15360]{2,1,0:T(2,128)(2,1)}), bf16[32,2,15360]{2,1,0:T(2,128)(2,1)S(1)}, u32[]{:S(2)}, u32[]{:S(2)}) async-start(bf16[32,2,15360]{2,1,0:T(2,128)(2,1)} %reshape.113), calls=%async_computation.2 | async-start | bytes 3932160 | tf_op jit(solution)/shard_map/all_to_all | solution.py:122
  639.3 1.9 copy-start.3
  639.3 2.5 copy-start.7
  641.8 26.6 %copy-start.1 = (bf16[1024,1024]{1,0:T(8,128)(2,1)S(1)}, bf16[1024,1024]{1,0:T(8,128)(2,1)}, u32[]{:S(2)}) copy-start(bf16[1024,1024]{1,0:T(8,128)(2,1)} %param.20) | copy-start | bytes 6291460
Sparse Core Ops, SparseCore 0:
  33.1 83.7 all-gather.3
  176.1 177.2 all-gather.5
where the time goes:
time: 682 us; the launch traced here: 675 us
  waiting for transfers between devices  269 us (39%)
  local copies, waits for them, and re-layouts  168 us (25%)
  matrix products  132 us (19%)
  blocking collectives  51.8 us (8%)
  other arithmetic  21.3 us (3%)
  starting transfers between devices  18.9 us (3%)
  between operations  14 us (2%)
    all_to_all x1, waiting for transfers between devices, local(): lax.all_to_all(spatial_proj, ('band', 'pix'), split_axis=1, concat_axis=0...  240 us
    squeeze x60, local copies, waits for them, and re-layouts, local(): attended = jnp.moveaxis(lax.map(one_item, per_item), 0, 1)[:, None]  54.8 us
    all_gather x1, blocking collectives, local(): bias_piece = lax.all_gather(up_bias, 'pix', axis=0, tiled=True)  51.8 us
    dot_general x61, matrix products, attend(): jnp.einsum(form_mix, probabilities, value_rows, preferred_element_type=jn...  50.8 us
    reshape x2, local copies, waits for them, and re-layouts, local(): spatial_proj.reshape(pixel_count, group_count, items_each, 3 * head_dim)  27 us
    dot_general x1, matrix products, local(): jnp.dot(hidden, down_piece, preferred_element_type=jnp.float32)  26.6 us
    all_to_all x1, waiting for transfers between devices, local(): lax.all_to_all(local_tokens, 'band', split_axis=0, concat_axis=1, tiled=T...  23.7 us
    dot_general x61, matrix products, attend(): jnp.einsum(form_scores, queries, key_rows, preferred_element_type=jnp.flo...  17.7 us
  transfers between devices with their start and end apart: 7, of which 3 were waited for; matrix products, arithmetic and copies ran while one was open for 42% of the time, Pallas kernels for 0%

commit v1 on v0

v1 whole, which is shorter than its diff:
```python
import functools

import jax
import jax.numpy as jnp
from jax import lax
from jax.experimental import pallas as pl
from jax.experimental.pallas import tpu as pltpu
from jax.sharding import PartitionSpec as P

HEADS = 16
CH_TOK = 16
WIN = 2 * CH_TOK
LANES = 128
GROUP = LANES // WIN
SPAN = LANES // CH_TOK
F32 = jnp.float32
BF16 = jnp.bfloat16
HIGH = lax.Precision.HIGHEST


def mm(a, b):
    return jnp.dot(a, b, preferred_element_type=F32)


def mm_t(a, b):
    return lax.dot_general(a, b, (((1,), (1,)), ((), ())), preferred_element_type=F32)


def split2(x):
    hi = x.astype(BF16)
    return hi, (x - hi.astype(F32)).astype(BF16)


def spectral_kernel(
    px,
    nb,
    bands,
    base_ref,
    rad_ref,
    sel4_ref,
    sel1_ref,
    gram_ref,
    cross_ref,
    place_ref,
    const_ref,
    mse_ref,
    mee_ref,
    msw_ref,
    mew_ref,
    av_ref,
    stem_ref,
    embed_ref,
    out_w_ref,
    out_ref,
    win,
    ue,
    uw,
    rstd,
):
    base = base_ref[0]
    hg_count = HEADS // GROUP
    tiles = bands // SPAN
    lane = lax.broadcasted_iota(jnp.int32, (px, LANES), 1)
    acc = jnp.zeros((px, LANES), F32)
    for j in range(tiles):
        block = rad_ref[:, j * LANES : (j + 2) * LANES]
        wide = mm(block, sel4_ref[...])
        for i in range(SPAN):
            t = j * SPAN + i
            win[t * px : (t + 1) * px, :] = wide[:, i * LANES : (i + 1) * LANES]
        thin = mm(block, sel1_ref[...])
        thin_b = thin.astype(BF16)
        prod = thin * (
            mm(thin_b, gram_ref[0]) + mm(thin_b, gram_ref[1]) + cross_ref[j : j + 1, :]
        )
        hi, lo = split2(prod)
        summed = mm(hi, place_ref[...]) + mm(lo, place_ref[...])
        acc = jnp.where(lane // SPAN == j, summed, acc)
    for t in range(bands, LANES):
        win[t * px : (t + 1) * px, :] = jnp.zeros((px, LANES), F32)
    scale = lax.rsqrt(acc + const_ref[...] + 1e-5)
    rstd[...] = scale

    own = []
    for i in range(nb):
        rows = pl.ds(pl.multiple_of((base + i) * px, px), px)
        mine = win[rows, :].astype(BF16)
        own.append(mine)
        rq = jnp.sum(jnp.where(lane == base + i, scale, 0.0), axis=1, keepdims=True)
        part = (mm(mine, mse_ref[...]) + mee_ref[i : i + 1, :]) * rq
        for k in range(HEADS):
            r = k * nb + i
            ue[r * px : (r + 1) * px, :] = part[:, k * LANES : (k + 1) * LANES]
        part = (mm(mine, msw_ref[...]) + mew_ref[i : i + 1, :]) * rq
        for hl in range(GROUP):
            for hg in range(hg_count):
                r = (hl * hg_count + hg) * nb + i
                piece = part[:, hg * LANES : (hg + 1) * LANES]
                uw[r * px : (r + 1) * px, :] = jnp.where(lane // WIN == hl, piece, 0.0)

    rows = HEADS * nb
    valid = lax.broadcasted_iota(jnp.int32, (rows, LANES), 1) < bands
    step = 8

    def pixels(g, _):
        ps = [g * step + i for i in range(step)]
        ws = [win[pl.ds(p, LANES, stride=px), :].astype(BF16) for p in ps]
        ls = [uw[pl.ds(p, rows, stride=px), :].astype(BF16) for p in ps]
        rk = rstd[pl.ds(pl.multiple_of(g * step, step), step), :]
        ss = [mm_t(a, w) for a, w in zip(ls, ws)]
        es = []
        for i, p in enumerate(ps):
            rki = rk[i : i + 1, :]
            s = (ss[i] + ue[pl.ds(p, rows, stride=px), :]) * rki
            s = jnp.where(valid, s, -1e30)
            e = jnp.exp(s - jnp.max(s, axis=1, keepdims=True))
            e = e * (1.0 / jnp.sum(e, axis=1, keepdims=True))
            es.append(e * rki)
        zs = [mm(e.astype(BF16), w) for e, w in zip(es, ws)]
        for i, p in enumerate(ps):
            ue[pl.ds(p, rows, stride=px), :] = es[i]
            uw[pl.ds(p, rows, stride=px), :] = zs[i]
        return 0

    lax.fori_loop(0, px // step, pixels, 0)

    wide_lane = lax.broadcasted_iota(jnp.int32, (nb * px, LANES), 1)
    mixes = []
    for hg in range(hg_count):
        parts = []
        z = jnp.zeros((nb * px, LANES), F32)
        for hl in range(GROUP):
            r = (hl * hg_count + hg) * nb * px
            parts.append(ue[r : r + nb * px, :].astype(BF16))
            z = jnp.where(wide_lane // WIN == hl, uw[r : r + nb * px, :], z)
        parts.append(z.astype(BF16))
        mixes.append(mm(jnp.concatenate(parts, axis=1), av_ref[hg]).astype(BF16))
    update = mm(jnp.concatenate(mixes, axis=1), out_w_ref[...])
    for i in range(nb):
        token = (mm(own[i], stem_ref[...]) + embed_ref[i : i + 1, :]).astype(BF16)
        out_ref[i] = token.astype(F32) + update[i * px : (i + 1) * px, :]


def spatial_kernel(x_ref, gain_ref, qkv_ref, w_ref, out_ref, proj, mixed):
    x = x_ref[0]
    pixels, width = x.shape
    mean = jnp.mean(x, axis=1, keepdims=True)
    cent = x - mean
    var = jnp.mean(cent * cent, axis=1, keepdims=True)
    normed = (cent * lax.rsqrt(var + 1e-5) * gain_ref[...]).astype(BF16)
    chunk = 768
    for c in range(0, 3 * width, chunk):
        proj[:, c : c + chunk] = mm(normed, qkv_ref[:, c : c + chunk]).astype(BF16)
    head = width // HEADS
    lane = lax.broadcasted_iota(jnp.int32, (pixels, 2 * head), 1)
    low = lane < head
    for pair in range(HEADS // 2):
        c = pair * 6 * head
        t0 = proj[:, c : c + 2 * head]
        t1 = proj[:, c + 2 * head : c + 4 * head]
        t2 = proj[:, c + 4 * head : c + 6 * head]
        zero = jnp.zeros_like(t0)
        r0 = jnp.concatenate([t0[:, head:], t0[:, :head]], axis=1)
        r2 = jnp.concatenate([t2[:, head:], t2[:, :head]], axis=1)
        outs = []
        for q, k, v in (
            (jnp.where(low, t0, zero), r0, t1),
            (jnp.where(low, zero, t1), r2, t2),
        ):
            s = mm_t(q, k)
            e = jnp.exp((s - jnp.max(s, axis=1, keepdims=True)) * (head**-0.5))
            total = jnp.sum(e, axis=1, keepdims=True)
            outs.append(mm(e.astype(BF16), v) * (1.0 / total))
        mixed[:, pair * 2 * head : (pair + 1) * 2 * head] = jnp.where(
            low, outs[0], outs[1]
        ).astype(BF16)
    out_ref[0] = (x + mm(mixed[...], w_ref[...])).astype(BF16)


def flip_order(parts, index):
    out = jnp.stack(parts)
    bit = 1
    while bit < len(parts):
        shaped = out.reshape((len(parts) // (2 * bit), 2, bit) + out.shape[1:])
        turned = shaped[:, ::-1].reshape(out.shape)
        out = jnp.where((index // bit) % 2 == 1, turned, out)
        bit *= 2
    return out


def swap(x, axis, mask):
    count = lax.axis_size(axis)
    return lax.ppermute(x, axis, [(i, i ^ mask) for i in range(count)])


def gather_radiance(radiance):
    pix, band = lax.axis_index("pix"), lax.axis_index("band")
    r = radiance.astype(BF16)
    half = lax.axis_size("pix") // 2
    zs = flip_order([r] + [swap(r, "pix", 2 * k) for k in range(1, half)], pix // 2)
    bs = flip_order(
        [zs] + [swap(zs, "band", k) for k in range(1, lax.axis_size("band"))], band
    )
    cs = flip_order([bs, swap(bs, "pix", 1)], pix % 2)
    full = cs.transpose(2, 0, 3, 1, 4)
    rows = full.shape[0] * full.shape[1] * full.shape[2]
    return full.reshape(rows, full.shape[3] * full.shape[4])


def layer_norm(values, scaling):
    values = values.astype(F32)
    centred = values - jnp.mean(values, axis=-1, keepdims=True)
    variance = jnp.mean(centred * centred, axis=-1, keepdims=True)
    return centred * lax.rsqrt(variance + 1e-05) * scaling


def spectral_tables(stem_weight, band_embed, gain, qkv, base, nb):
    bands, width = band_embed.shape
    head = width // HEADS
    hg = HEADS // GROUP
    stem_c = stem_weight - jnp.mean(stem_weight, axis=1, keepdims=True)
    emb_c = band_embed - jnp.mean(band_embed, axis=1, keepdims=True)
    feats = (jnp.concatenate([stem_c, emb_c]) * gain).astype(BF16)
    a = mm(feats, qkv).astype(BF16).reshape(WIN + bands, HEADS, 3, head)
    aq, ak, av = a[:, :, 0], a[:, :, 1], a[:, :, 2]
    mine = jnp.concatenate([aq[:WIN], lax.dynamic_slice_in_dim(aq, WIN + base, nb, 0)])
    m = jnp.einsum("ihd,jhd->ihj", mine, ak, preferred_element_type=F32) * head**-0.5
    m = m.reshape(WIN + nb, hg, GROUP, WIN + bands)
    me = jnp.pad(m[..., WIN:], ((0, 0),) * 3 + ((0, LANES - bands),))
    me = me.transpose(0, 2, 1, 3).reshape(WIN + nb, HEADS * LANES)
    mw = m[..., :WIN].reshape(WIN + nb, hg * LANES)

    def stacked(x, n):
        pieces, rest = [], x
        for _ in range(n):
            hi, rest = rest.astype(BF16), rest - rest.astype(BF16).astype(F32)
            pieces.append(hi)
        return jnp.pad(jnp.concatenate(pieces), ((0, LANES - n * WIN), (0, 0)))

    eye = jnp.eye(GROUP, dtype=BF16)
    ave = jnp.pad(av[WIN:], ((0, LANES - bands), (0, 0), (0, 0))).reshape(LANES, hg, GROUP, head)
    ave = jnp.einsum("tgld,lm->gltmd", ave, eye).reshape(hg, GROUP * LANES, GROUP * head)
    avw = av[:WIN].reshape(WIN, hg, GROUP, head)
    avw = jnp.einsum("cgld,lm->glcmd", avw, eye).reshape(hg, LANES, GROUP * head)
    gram = jnp.dot(stem_c, stem_c.T, precision=HIGH) / width
    gram = jnp.kron(jnp.eye(SPAN, dtype=F32), gram)
    cross = 2.0 * jnp.dot(emb_c, stem_c.T, precision=HIGH) / width
    const = jnp.pad(jnp.mean(emb_c * emb_c, axis=1), (0, LANES - bands))[None]
    return dict(
        mse=stacked(me[:WIN], 2),
        mee=me[WIN:],
        msw=stacked(mw[:WIN], 2),
        mew=mw[WIN:],
        av=jnp.concatenate([ave, avw], axis=1),
        stem=stacked(stem_weight, 3),
        embed=lax.dynamic_slice_in_dim(band_embed, base, nb, 0),
        gram=jnp.stack(split2(gram)),
        cross=cross.reshape(bands // SPAN, SPAN * WIN),
        const=const,
    )


def selectors():
    row = jnp.arange(2 * LANES)[:, None]
    col = jnp.arange(SPAN * LANES)[None]
    sel4 = (row == (col // LANES) * CH_TOK + col % WIN).astype(BF16)
    col = jnp.arange(SPAN * WIN)[None]
    sel1 = (row == (col // WIN) * CH_TOK + col % WIN).astype(BF16)
    place = (row // WIN == jnp.arange(LANES)[None] % SPAN).astype(BF16)
    return sel4, sel1, place


def whole_spec(shape):
    return pl.BlockSpec(shape, lambda *_: (0,) * len(shape))


def spectral(full, base, tables, spec_out, nb, bands):
    pixels, channels = full.shape
    width = spec_out.shape[0]
    edge = CH_TOK // 2
    lanes = (bands // SPAN + 1) * LANES
    rad = jnp.pad(full, ((0, 0), (edge, lanes - channels - edge)))
    px = 64
    sel4, sel1, place = selectors()
    t = tables
    consts = [
        sel4, sel1, t["gram"], t["cross"], place, t["const"], t["mse"], t["mee"],
        t["msw"], t["mew"], t["av"], t["stem"], t["embed"], spec_out,
    ]
    return pl.pallas_call(
        functools.partial(spectral_kernel, px, nb, bands),
        grid=(pixels // px,),
        out_shape=jax.ShapeDtypeStruct((nb, pixels, width), F32),
        in_specs=[pl.BlockSpec(memory_space=pltpu.SMEM), pl.BlockSpec((px, lanes), lambda i: (i, 0))]
        + [whole_spec(c.shape) for c in consts],
        out_specs=pl.BlockSpec((nb, px, width), lambda i: (0, i, 0)),
        scratch_shapes=[
            pltpu.VMEM((LANES * px, LANES), F32),
            pltpu.VMEM((HEADS * nb * px, LANES), F32),
            pltpu.VMEM((HEADS * nb * px, LANES), F32),
            pltpu.VMEM((px, LANES), F32),
        ],
        compiler_params=pltpu.CompilerParams(vmem_limit_bytes=56 * 2**20),
        name="spectral",
    )(base[None], rad, *consts)


def spatial(x, gain, qkv, w):
    nb, pixels, width = x.shape
    return pl.pallas_call(
        spatial_kernel,
        grid=(nb,),
        out_shape=jax.ShapeDtypeStruct(x.shape, BF16),
        in_specs=[
            pl.BlockSpec((1, pixels, width), lambda i: (i, 0, 0)),
            whole_spec((1, width)),
            whole_spec(qkv.shape),
            whole_spec(w.shape),
        ],
        out_specs=pl.BlockSpec((1, pixels, width), lambda i: (i, 0, 0)),
        scratch_shapes=[
            pltpu.VMEM((pixels, 3 * width), BF16),
            pltpu.VMEM((pixels, width), BF16),
        ],
        compiler_params=pltpu.CompilerParams(vmem_limit_bytes=56 * 2**20),
        name="spatial",
    )(x, gain[None], qkv, w)


def local(
    radiance,
    stem_weight,
    band_embed,
    norm_spectral,
    spec_qkv,
    spec_out,
    norm_spatial,
    spat_qkv,
    spat_out,
    norm_mlp,
    up_weight,
    up_bias,
    down_weight,
):
    bands, width = band_embed.shape
    bsize, psize = lax.axis_size("band"), lax.axis_size("pix")
    devices = bsize * psize
    nb = -(-bands // devices)
    band = lax.axis_index("band")
    place = lax.axis_index("pix") * bsize + band
    base = jnp.minimum(place * nb, bands - nb).astype(jnp.int32)

    share = up_weight.shape[0] // bsize
    both = jnp.concatenate(
        [
            lax.dynamic_slice_in_dim(up_weight, band * share, share, 0),
            lax.dynamic_slice_in_dim(down_weight, band * share, share, 0),
        ]
    )
    both = lax.all_gather(both, ("pix", "band"), axis=0)
    up = both[:, :share].reshape(-1, width)
    down = both[:, share:].reshape(-1, width)
    bias = lax.all_gather(up_bias, "pix", axis=0, tiled=True)

    full = gather_radiance(radiance)
    tables = spectral_tables(stem_weight, band_embed, norm_spectral, spec_qkv, base, nb)
    after_spectral = spectral(full, base, tables, spec_out, nb, bands)
    after_spatial = spatial(after_spectral, norm_spatial, spat_qkv, spat_out)
    moved = lax.all_to_all(
        after_spatial, ("pix", "band"), split_axis=1, concat_axis=0, tiled=True
    )[:bands]
    pixel_count = moved.shape[1]
    x = moved.reshape(-1, width).astype(F32)
    mlp_in = layer_norm(x, norm_mlp).astype(BF16)
    pre_act = mm_t(mlp_in, up) + bias.astype(F32)
    hidden = jax.nn.gelu(pre_act, approximate=True).astype(BF16)
    encoded = (x + mm(hidden, down)).astype(BF16)
    return encoded.reshape(bands, pixel_count, width).transpose(1, 0, 2)


def solution(mesh):
    placed = (
        P("pix", "band"),
        P(),
        P(),
        P(),
        P(),
        P(),
        P(),
        P(),
        P(),
        P(),
        P("pix", None),
        P("pix"),
        P("pix", None),
    )
    return jax.shard_map(
        local, mesh=mesh, in_specs=placed, out_specs=P(("pix", "band"), None, None), check_vma=False
    )
```

time: 682 us -> 298 us (0.44)
  waiting for transfers between devices: 269 us -> 7.7 us
  local copies, waits for them, and re-layouts: 168 us -> 45.3 us
  matrix products: 132 us -> 30.8 us
  Pallas kernels: 0 us -> 96.7 us
    all_to_all x3 -> x1, waiting for transfers between devices: 264 us -> 0.01 us  [local(): lax.all_to_all(after_spatial, ('pix', 'band'), split_axis=1, concat_axis=...]
    dot_general x128 -> x5, matrix products: 132 us -> 30.8 us  [the longest x2 29.8 us: mm(): return jnp.dot(a, b, preferred_element_type=F32)]
    pallas_call x0 -> x2, Pallas kernels: none -> 96.7 us  [the longest x1 72.3 us: spectral(): pl.pallas_call(functools.partial(spectral_kernel, px, nb, bands), grid=(p...]
    squeeze x60 -> x0, local copies, waits for them, and re-layouts: 54.8 us -> none  [local(): attended = jnp.moveaxis(lax.map(one_item, per_item), 0, 1)[:, None]]
    reshape x5 -> x7, local copies, waits for them, and re-layouts: 49.5 us -> 8.01 us  [the longest x1 3.89 us: local(): return encoded.reshape(bands, pixel_count, width).transpose(1, 0, 2)]
    convert_element_type x4 -> x3, local copies, waits for them, and re-layouts: 18.8 us -> 3.09 us  [the longest x1 2.24 us: local(): x = moved.reshape(-1, width).astype(F32)]
    slice x3 -> x14, local copies, waits for them, and re-layouts: 4.59 us -> 19.4 us  [the longest x1 11.9 us: local(): up = both[:, :share].reshape(-1, width)]
    unnamed x21, local copies, waits for them, and re-layouts: 15.4 us -> 2.49 us
  transfers between devices with their start and end apart: 7 -> 9, of which waited for: 3 -> 3; matrix products, arithmetic and copies ran while one was open for 42% -> 19% of each run, Pallas kernels for 0% -> 33%
where the time goes in v1:
time: 298 us; the launch traced here: 292 us
  Pallas kernels  96.7 us (32%)
  blocking collectives  54.8 us (18%)
  local copies, waits for them, and re-layouts  45.3 us (15%)
  matrix products  30.8 us (10%)
  other arithmetic  22.2 us (7%)
  starting transfers between devices  20.9 us (7%)
  between operations  14.1 us (5%)
  waiting for transfers between devices  7.7 us (3%)
    pallas_call x1, Pallas kernels, spectral(): pl.pallas_call(functools.partial(spectral_kernel, px, nb, bands), grid=(p...  72.3 us
    all_gather x1, blocking collectives, local(): bias = lax.all_gather(up_bias, 'pix', axis=0, tiled=True)  54.8 us
    dot_general x2, matrix products, mm(): return jnp.dot(a, b, preferred_element_type=F32)  29.8 us
    pallas_call x1, Pallas kernels, spatial(): pl.pallas_call(spatial_kernel, grid=(nb,), out_shape=jax.ShapeDtypeStruct...  24.3 us
    slice x1, local copies, waits for them, and re-layouts, local(): up = both[:, :share].reshape(-1, width)  11.9 us
    all_to_all x1, starting transfers between devices, local(): lax.all_to_all(after_spatial, ('pix', 'band'), split_axis=1, concat_axis=...  11.7 us
    ppermute x7, starting transfers between devices, swap(): return lax.ppermute(x, axis, [(i, i ^ mask) for i in range(count)])  9.25 us
    ppermute x7, waiting for transfers between devices, swap(): return lax.ppermute(x, axis, [(i, i ^ mask) for i in range(count)])  7.68 us
  transfers between devices with their start and end apart: 9, of which 3 were waited for; matrix products, arithmetic and copies ran while one was open for 19% of the time, Pallas kernels for 33%

profile of v1, /device:TPU:0, one launch (start us, length us, event | category | flops | bytes accessed | tf_op | source)
XLA Modules:
  0.0 292.4 jit_solution(11685580765858668223)
XLA Ops:
  6.5 1.1 constant_dynamic-slice_fusion
  8.5 1.5 convert_element_type.137
  10.0 5.0 %collective-permute-start.2 = (bf16[32,480]{1,0:T(8,128)(2,1)}, bf16[32,480]{1,0:T(8,128)(2,1)}, u32[]{:S(2)}, u32[]{:S(2)}) collective-permute-start(bf16[32,480]{1,0:T(8,128)(2,1)} %convert_element_type.137), channel_id=1, source_target_pairs={{0,6},{1,7},{2,4},{3,5},{4,2},{5,3},{6,0},{7,1},{8,14},{9,15},{10,... | collective-permute-start | bytes 92168 | tf_op jit(solution)/shard_map/ppermute | solution.py:193
  15.6 1.0 reduce_sum.45
  16.6 1.2 reduce_sum.46
  17.8 1.7 fusion.66
  19.7 4.3 %convolution_convert_fusion = bf16[152,3072]{1,0:T(8,128)(2,1)S(1)} fusion(bf16[1024,3072]{1,0:T(8,128)(2,1)} %param.17, f32[120,1024]{1,0:T(8,128)S(1)} %get-tuple-element.10, f32[32,1024]{1,0:T(8,128)S(1)} %get-tuple-element.19, f32[1024]{0:T(1024)S(1)} %copy-done.5), kind=kOutput, calls=%fused_computation.15 | convolution fusion | flops 957235200 | bytes 7852032 | tf_op jit(solution)/shard_map/dot_general | solution.py:22
  28.3 1.0 mul.141
  29.4 1.2 copy.76
  31.4 1.1 copy.77
  33.4 1.1 copy.67
  34.9 1.0 reshape.615
  37.9 1.5 constant_dynamic-slice_fusion.2.embed_ref
  40.9 1.1 subtract_convert_fusion.1
  42.8 1.6 fusion.32.stem_ref
  44.4 1.1 pad_maximum_fusion.av_ref
  47.2 0.9 fusion.21.sel4_ref
  53.9 2.7 collective-permute-start.5
  58.3 5.3 %collective-permute-done.5 = bf16[4,32,480]{2,1,0:T(8,128)(2,1)S(1)} collective-permute-done((bf16[4,32,480]{2,1,0:T(8,128)(2,1)S(1)}, bf16[4,32,480]{2,1,0:T(8,128)(2,1)S(1)}, u32[]{:S(2)}, u32[]{:S(2)}) %collective-permute-start.5) | collective-permute-done | bytes 122912 | tf_op jit(solution)/shard_map/ppermute | solution.py:193
  63.6 1.3 collective-permute-done.3
  66.3 1.1 collective-permute-done.6
  68.5 1.2 reshape.606
  69.8 1.4 pad.28.rad_ref
  71.2 72.3 %spectral.1.x_ref = f32[4,256,1024]{2,1,0:T(8,128)} custom-call(s32[1]{0:T(128)} %bitcast.base_ref, bf16[256,2048]{1,0:T(8,128)(2,1)} %pad.28.rad_ref, bf16[256,1024]{1,0:T(8,128)(2,1)} %fusion.21.sel4_ref, bf16[256,256]{1,0:T(8,128)(2,1)} %fusion.35.sel1_ref, bf16[2,256,256]{2,1,0:T(8,128)(2,1)} %pad_maximum_fusion.4.gram_ref, ...), custom_call_target="tpu_custom_call" | custom-call | tf_op jit(solution)/shard_map/spectral/pallas_call | solution.py:290
  143.5 24.3 %spatial.1 = bf16[4,256,1024]{2,1,0:T(8,128)(2,1)} custom-call(f32[4,256,1024]{2,1,0:T(8,128)} %spectral.1.x_ref, f32[1,1024]{1,0:T(1,128)} %bitcast.147, bf16[1024,3072]{1,0:T(8,128)(2,1)} %qkv_ref.1, bf16[1024,1024]{1,0:T(8,128)(2,1)} %w_ref.1), custom_call_target="tpu_custom_call" | custom-call | tf_op jit(solution)/shard_map/spatial/pallas_call | solution.py:310
  167.8 4.6 %copy.69 = bf16[4,256,1024]{2,0,1:T(4,128)(2,1)} copy(bf16[4,256,1024]{2,1,0:T(8,128)(2,1)} %spatial.1) | data formatting | bytes 4194304 | tf_op jit(solution)/shard_map/spatial/pallas_call | solution.py:310
  172.4 11.7 %all-to-all-start = ((bf16[4,256,1024]{2,0,1:T(4,128)(2,1)}), bf16[4,256,1024]{2,0,1:T(4,128)(2,1)S(1)}, u32[]{:S(2)}, u32[]{:S(2)}) async-start(bf16[4,256,1024]{2,0,1:T(4,128)(2,1)} %copy.69), calls=%async_computation | async-start | bytes 4194304 | tf_op jit(solution)/shard_map/all_to_all | solution.py:369
  184.1 54.8 %all-gather.1 = bf16[8,1,512]{2,1,0:T(2,128)(2,1)S(1)} all-gather(bf16[1,1,512]{2,1,0:T(2,128)(2,1)S(1)} %reshape.621), channel_id=1, replica_groups=mesh['band'=4,'pix'=8] {'pix'}, dimensions={0}, use_global_device_ids=true | all-gather | bytes 9216 | tf_op jit(solution)/shard_map/all_gather | solution.py:363
  241.9 2.2 copy.71
  244.1 11.9 %fusion.64 = (bf16[32,128,1024]{2,1,0:T(8,128)(2,1)}, bf16[32,128,1024]{2,1,0:T(8,128)(2,1)}) fusion(bf16[32,256,1024]{2,1,0:T(8,128)(2,1)} %bitcast.110), kind=kLoop, calls=%fused_computation.126 | loop fusion | bytes 33554432 | tf_op jit(solution)/shard_map/slice | solution.py:361
  256.0 25.5 %fusion.15 = bf16[120,8,1024]{2,1,0:T(8,128)(2,1)} fusion(bf16[4096,1024]{1,0:T(8,128)(2,1)} %bitcast.115, f32[4096]{0:T(1024)S(1)} %bitcast.146, bf16[960,1024]{1,0:T(8,128)(2,1)S(1)} %bitcast.129, bf16[4096,1024]{1,0:T(8,128)(2,1)} %bitcast.114, f32[30,4,8,1024]{3,2,1,0:T(8,128)} %copy.71), kind=kOutput, calls=%fused_computation.19 | convolution fusion | flops 16147415040 | bytes 24657920 | tf_op jit(solution)/shard_map/dot_general | solution.py:22
  281.5 3.9 %copy.82 = bf16[120,8,1024]{2,0,1:T(8,128)(2,1)} copy(bf16[120,8,1024]{2,1,0:T(8,128)(2,1)} %fusion.15) | data formatting | bytes 3932160 | tf_op jit(solution)/shard_map/reshape | solution.py:378
  (105 shorter events, 26.7 us)
Async XLA Ops:
  6.5 13.0 %copy-start.1 = (f32[120,1024]{1,0:T(8,128)S(1)}, f32[120,1024]{1,0:T(8,128)}, u32[]{:S(2)}) copy-start(f32[120,1024]{1,0:T(8,128)} %param.15) | copy-start | bytes 1474564
  6.5 13.2 %copy-start.5 = (f32[1024]{0:T(1024)S(1)}, f32[1024]{0:T(1024)}, u32[]{:S(2)}) copy-start(f32[1024]{0:T(1024)} %param.16) | copy-start | bytes 12292
  6.5 237.6 %all-gather.4.cloned.1.call-start = ((), (), s32[]{:S(2)}) async-start(), calls=%async_computation.1 | async-start | bytes 17301504 | tf_op jit(solution)/shard_map/all_gather | solution.py:360
  10.0 42.2 %collective-permute-start.2 = (bf16[32,480]{1,0:T(8,128)(2,1)}, bf16[32,480]{1,0:T(8,128)(2,1)}, u32[]{:S(2)}, u32[]{:S(2)}) collective-permute-start(bf16[32,480]{1,0:T(8,128)(2,1)} %convert_element_type.137), channel_id=1, source_target_pairs={{0,6},{1,7},{2,4},{3,5},{4,2},{5,3},{6,0},{7,1},{8,14},{9,15},{10,... | collective-permute-start | bytes 92168 | tf_op jit(solution)/shard_map/ppermute | solution.py:193
  15.0 37.1 %collective-permute-start.1 = (bf16[32,480]{1,0:T(8,128)(2,1)}, bf16[32,480]{1,0:T(8,128)(2,1)}, u32[]{:S(2)}, u32[]{:S(2)}) collective-permute-start(bf16[32,480]{1,0:T(8,128)(2,1)} %convert_element_type.137), channel_id=1, source_target_pairs={{0,4},{1,5},{2,6},{3,7},{4,0},{5,1},{6,2},{7,3},{8,12},{9,13},{10,... | collective-permute-start | bytes 92168 | tf_op jit(solution)/shard_map/ppermute | solution.py:193
  15.0 37.1 %collective-permute-start = (bf16[32,480]{1,0:T(8,128)(2,1)}, bf16[32,480]{1,0:T(8,128)(2,1)}, u32[]{:S(2)}, u32[]{:S(2)}) collective-permute-start(bf16[32,480]{1,0:T(8,128)(2,1)} %convert_element_type.137), channel_id=1, source_target_pairs={{0,2},{1,3},{2,0},{3,1},{4,6},{5,7},{6,4},{7,5},{8,10},{9,11},{10,... | collective-permute-start | bytes 92168 | tf_op jit(solution)/shard_map/ppermute | solution.py:193
  26.3 1.7 copy-start
  36.2 8.2 %copy-start.2 = (bf16[4,128,256]{2,1,0:T(8,128)(2,1)S(1)}, bf16[4,128,256]{2,1,0:T(8,128)(2,1)}, u32[]{:S(2)}) copy-start(bf16[4,128,256]{2,1,0:T(8,128)(2,1)} %reshape.615) | copy-start | bytes 786436
  37.3 9.0 %copy-start.3 = (f32[32,2048]{1,0:T(8,128)S(1)}, f32[32,2048]{1,0:T(8,128)}, u32[]{:S(2)}) copy-start(f32[32,2048]{1,0:T(8,128)} %slice.72) | copy-start | bytes 786436
  37.9 8.4 %copy-start.4 = (f32[32,480]{1,0:T(8,128)S(1)}, f32[32,480]{1,0:T(8,128)}, u32[]{:S(2)}) copy-start(f32[32,480]{1,0:T(8,128)} %param.13) | copy-start | bytes 184324
  53.9 9.6 %collective-permute-start.5 = (bf16[4,32,480]{2,1,0:T(8,128)(2,1)S(1)}, bf16[4,32,480]{2,1,0:T(8,128)(2,1)S(1)}, u32[]{:S(2)}, u32[]{:S(2)}) collective-permute-start(bf16[4,32,480]{2,1,0:T(8,128)(2,1)S(1)} %fusion.41), channel_id=1, source_target_pairs={{0,24},{8,16},{16,8},{24,0},{1,25},{9,17},{17,9},{25,1},{2,26},{10... | collective-permute-start | bytes 368648 | tf_op jit(solution)/shard_map/ppermute | solution.py:193
  56.6 6.9 %collective-permute-start.4 = (bf16[4,32,480]{2,1,0:T(8,128)(2,1)S(1)}, bf16[4,32,480]{2,1,0:T(8,128)(2,1)S(1)}, u32[]{:S(2)}, u32[]{:S(2)}) collective-permute-start(bf16[4,32,480]{2,1,0:T(8,128)(2,1)S(1)} %fusion.41), channel_id=1, source_target_pairs={{0,16},{8,24},{16,0},{24,8},{1,17},{9,25},{17,1},{25,9},{2,18},{10... | collective-permute-start | bytes 368648 | tf_op jit(solution)/shard_map/ppermute | solution.py:193
  57.1 7.7 %collective-permute-start.3 = (bf16[4,32,480]{2,1,0:T(8,128)(2,1)S(1)}, bf16[4,32,480]{2,1,0:T(8,128)(2,1)S(1)}, u32[]{:S(2)}, u32[]{:S(2)}) collective-permute-start(bf16[4,32,480]{2,1,0:T(8,128)(2,1)S(1)} %fusion.41), channel_id=1, source_target_pairs={{0,8},{8,0},{16,24},{24,16},{1,9},{9,1},{17,25},{25,17},{2,10},{10... | collective-permute-start | bytes 368648 | tf_op jit(solution)/shard_map/ppermute | solution.py:193
  65.4 2.0 collective-permute-start.6
  167.8 16.3 %copy-start.7 = (bf16[512]{0:T(512)(128)(2,1)S(1)}, bf16[512]{0:T(512)(128)(2,1)}, u32[]{:S(2)}) copy-start(bf16[512]{0:T(512)(128)(2,1)} %param.24) | copy-start | bytes 3076
  172.4 66.5 %all-to-all-start = ((bf16[4,256,1024]{2,0,1:T(4,128)(2,1)}), bf16[4,256,1024]{2,0,1:T(4,128)(2,1)S(1)}, u32[]{:S(2)}, u32[]{:S(2)}) async-start(bf16[4,256,1024]{2,0,1:T(4,128)(2,1)} %copy.69), calls=%async_computation | async-start | bytes 4194304 | tf_op jit(solution)/shard_map/all_to_all | solution.py:369
  238.9 1.7 copy-start.6
Sparse Core Ops, SparseCore 0:
  10.2 120.5 all-gather.3
